TPU v7x, 512 devices: a whole 4x4x16 slice. The times are simulated.
512 devices in a mesh: dp: 8 (over y, core), seq: 64 (over x, z).
Axes of the slice: x: 4, y: 4, z: 16, core: 2. Of those that a mesh axis runs over, the one named last changes fastest.
Arguments:
- queries: bfloat16 [8, 16384, 384], P('dp', 'seq'), may hold values from -6 to 6
- keys: bfloat16 [8, 16384, 384], P('dp', 'seq'), may hold values from -6 to 6
- values: bfloat16 [8, 16384, 384], P('dp', 'seq'), may hold values from -6 to 6
- outputs: bfloat16 [8, 16384, 384], P('dp', 'seq'), may hold values from -16 to 16
- d_final: bfloat16 [8, 16384, 768], P('dp', 'seq'), may hold values from -6 to 6
- stats: float32 [8, 16384, 8], P('dp', 'seq'), may hold values from 6.5 to 8
- w_out: bfloat16 [384, 768], replicated, may hold values from -0.21875 to 0.21875
Outputs:
- d_queries: bfloat16 [8, 16384, 384], P('dp', 'seq')
- d_keys: bfloat16 [8, 16384, 384], P('dp', 'seq')
- d_values: bfloat16 [8, 16384, 384], P('dp', 'seq')
- grad_weight: float32 [384, 768], P('seq')
All inputs are finite; a program needn't handle non-finite values.
Results may differ from a plain program's by a relative error of at most 0.0057.
Values may be sent and summed in bfloat16 or wider, within the bound.
No kernel may reach another device: no remote copies, remote signals or barrier semaphores. Data moves between devices by JAX's collectives and lax.ppermute only.
A program may use at most 64 MiB of HBM per device.

v0:
```python
import jax
import jax.numpy as jnp
from jax import lax
from jax.sharding import PartitionSpec as P

GROUP = 8


def swapped(shard, axis, distance):
    return lax.ppermute(shard, axis, [(i, i ^ 1 << distance) for i in range(lax.axis_size(axis))])


def pick(x, stride, heads):
    shaped = x.reshape(x.shape[0] // stride, stride, heads, x.shape[-1])
    return jnp.stack([shaped[:, h % stride, h, :] for h in range(heads)], axis=1)


def place(y, stride, heads, rows):
    shaped = jnp.zeros((rows // stride, stride, heads, y.shape[-1]), jnp.float32)
    for h in range(heads):
        shaped = shaped.at[:, h % stride, h, :].set(y[:, h, :])
    return shaped.reshape(rows, heads, y.shape[-1])


def set_backward(query, d_out, lse, delta, keys, values, scale):
    scores = jnp.einsum("nhc,mhc->hnm", query, keys, preferred_element_type=jnp.float32) * scale
    probs = jnp.exp(scores - jnp.transpose(lse)[:, :, None])
    d_probs = jnp.einsum("nhc,mhc->hnm", d_out, values, preferred_element_type=jnp.float32)
    d_scores = (probs * (d_probs - jnp.transpose(delta)[:, :, None])).astype(jnp.bfloat16)
    probs_low = probs.astype(jnp.bfloat16)
    d_query = jnp.einsum("hnm,mhc->nhc", d_scores, keys, preferred_element_type=jnp.float32) * scale
    d_key = jnp.einsum("hnm,nhc->mhc", d_scores, query, preferred_element_type=jnp.float32) * scale
    d_value = jnp.einsum("hnm,nhc->mhc", probs_low, d_out, preferred_element_type=jnp.float32)
    return (d_query, d_key, d_value)


def group_collect(block, bits):
    where = lax.axis_index("seq")
    gathered = block
    for bit in range(bits):
        other = swapped(gathered, "seq", bit)
        high = where >> bit & 1
        gathered = jnp.where(
            high == 1,
            jnp.concatenate([other, gathered], axis=1),
            jnp.concatenate([gathered, other], axis=1),
        )
    return gathered


def group_return(grads, bits):
    where = lax.axis_index("seq")
    current = grads
    for bit in reversed(range(bits)):
        half = current.shape[1] // 2
        lower = current[:, :half]
        upper = current[:, half:]
        high = where >> bit & 1
        keep = jnp.where(high == 1, upper, lower)
        send = jnp.where(high == 1, lower, upper)
        current = keep + swapped(send, "seq", bit)
    return current


def on_device(queries, keys, values, outputs, d_final, stats, w_out):
    query2 = queries[0]
    key2 = keys[0]
    value2 = values[0]
    output2 = outputs[0]
    upstream = d_final[0]
    lse = stats[0]
    rows = query2.shape[0]
    width = query2.shape[1]
    heads = lse.shape[1]
    size = width // heads
    scale = float(size) ** (-0.5)
    seq_count = lax.axis_size("seq")
    d_out = lax.dot_general(
        upstream, w_out, (((1,), (1,)), ((), ())), preferred_element_type=jnp.float32
    ).astype(jnp.bfloat16)
    query3 = query2.reshape(rows, heads, size)
    key3 = key2.reshape(rows, heads, size)
    value3 = value2.reshape(rows, heads, size)
    dout3 = d_out.reshape(rows, heads, size)
    delta = jnp.sum(
        dout3.astype(jnp.float32) * output2.reshape(rows, heads, size).astype(jnp.float32), axis=-1
    )
    full = lax.dot_general(
        output2, upstream, (((0,), (0,)), ((), ())), preferred_element_type=jnp.float32
    )
    summed = lax.psum(full, "dp")
    grad_weight = lax.psum_scatter(summed, "seq", scatter_dimension=0, tiled=True)
    dq0, dk0, dv0 = set_backward(query3, dout3, lse, delta, key3, value3, scale)
    total_q = dq0
    total_k = dk0
    total_v = dv0

    def level_inputs(stride):
        return (
            pick(query3, stride, heads),
            pick(dout3, stride, heads),
            pick(lse[:, :, None], stride, heads)[..., 0],
            pick(delta[:, :, None], stride, heads)[..., 0],
            pick(key3, stride, heads),
            pick(value3, stride, heads),
        )

    group_bits = GROUP.bit_length() - 1
    pq, pd, pl, pdl, pk, pv = level_inputs(GROUP)
    count = rows // GROUP
    pair = jnp.stack([pk.reshape(count, width), pv.reshape(count, width)])
    remote = group_collect(pair, group_bits)
    dq1, dk1, dv1 = set_backward(
        pq,
        pd,
        pl,
        pdl,
        remote[0].reshape(-1, heads, size),
        remote[1].reshape(-1, heads, size),
        scale,
    )
    back = group_return(jnp.stack([dk1.reshape(-1, width), dv1.reshape(-1, width)]), group_bits)
    total_q = total_q + place(dq1, GROUP, heads, rows)
    total_k = total_k + place(back[0].reshape(count, heads, size), GROUP, heads, rows)
    total_v = total_v + place(back[1].reshape(count, heads, size), GROUP, heads, rows)
    fq, fd, fl, fdl, fk, fv = level_inputs(seq_count)
    far_count = rows // seq_count
    far_pair = jnp.stack([fk.reshape(far_count, width), fv.reshape(far_count, width)])
    far_remote = lax.all_gather(far_pair, "seq", axis=1, tiled=True)
    dq2, dk2, dv2 = set_backward(
        fq,
        fd,
        fl,
        fdl,
        far_remote[0].reshape(-1, heads, size),
        far_remote[1].reshape(-1, heads, size),
        scale,
    )
    far_terms = jnp.stack([dk2.reshape(-1, width), dv2.reshape(-1, width)])
    far_back = lax.psum_scatter(far_terms, "seq", scatter_dimension=1, tiled=True)
    total_q = total_q + place(dq2, seq_count, heads, rows)
    total_k = total_k + place(far_back[0].reshape(far_count, heads, size), seq_count, heads, rows)
    total_v = total_v + place(far_back[1].reshape(far_count, heads, size), seq_count, heads, rows)
    d_queries = total_q.reshape(1, rows, width).astype(jnp.bfloat16)
    d_keys = total_k.reshape(1, rows, width).astype(jnp.bfloat16)
    d_values = total_v.reshape(1, rows, width).astype(jnp.bfloat16)
    return (d_queries, d_keys, d_values, grad_weight)


def solution(mesh):
    placed = (
        P("dp", "seq", None),
        P("dp", "seq", None),
        P("dp", "seq", None),
        P("dp", "seq", None),
        P("dp", "seq", None),
        P("dp", "seq", None),
        P(),
    )
    return jax.shard_map(
        on_device,
        mesh=mesh,
        in_specs=placed,
        out_specs=(
            P("dp", "seq", None),
            P("dp", "seq", None),
            P("dp", "seq", None),
            P("seq", None),
        ),
        check_vma=False,
    )
```

profile of v0, /device:TPU:8, one launch (start us, length us, event | category | flops | bytes accessed | tf_op | source)
XLA Modules:
  0.0 632.5 jit_solution(2512236024374545083)
XLA Ops:
  8.8 158.2 %fusion = f32[8,768]{1,0:T(8,128)} fusion(f32[384,768]{1,0:T(8,128)S(1)} %fusion.28), kind=kCustom, calls=%all-reduce-scatter | all-reduce-scatter fusion | flops 393217 | bytes 1206272
  181.1 98.5 %all_gather.3 = bf16[2,256,384]{2,0,1:T(2,128)(2,1)S(1)} all-gather(bf16[2,4,384]{2,0,1:T(2,128)(2,1)S(1)} %copy.1023), channel_id=1, replica_groups=mesh['dp'=8,'seq'=64] {'seq'}, dimensions={1}, use_global_device_ids=true | all-gather | bytes 399360 | tf_op jit(solution)/shard_map/all_gather | solution.py:129
  298.7 3.0 collective-permute-start.21
  303.2 4.5 collective-permute-start.16
  307.8 9.6 %collective-permute-start.15 = (f32[8,768]{1,0:T(8,128)}, f32[8,768]{1,0:T(8,128)S(1)}, u32[]{:S(2)}, u32[]{:S(2)}) collective-permute-start(f32[8,768]{1,0:T(8,128)} %fusion), channel_id=1, source_target_pairs={{0,10},{1,11},{2,12},{3,13},{4,14},{5,15},{6,16},{7,17},{8,18},{9,... | collective-permute-start | bytes 73736
  317.4 2.6 collective-permute-start.1
  320.7 7.0 %collective-permute-start.14 = (f32[8,768]{1,0:T(8,128)}, f32[8,768]{1,0:T(8,128)S(1)}, u32[]{:S(2)}, u32[]{:S(2)}) collective-permute-start(f32[8,768]{1,0:T(8,128)} %fusion), channel_id=1, source_target_pairs={{0,9},{1,10},{2,11},{3,12},{4,13},{5,14},{6,15},{7,16},{8,17},{9,1... | collective-permute-start | bytes 73736
  327.7 7.8 %collective-permute-start.13 = (f32[8,768]{1,0:T(8,128)}, f32[8,768]{1,0:T(8,128)S(1)}, u32[]{:S(2)}, u32[]{:S(2)}) collective-permute-start(f32[8,768]{1,0:T(8,128)} %fusion), channel_id=1, source_target_pairs={{0,8},{1,9},{2,10},{3,11},{4,12},{5,13},{6,14},{7,15},{8,16},{9,17... | collective-permute-start | bytes 73736
  335.5 4.9 collective-permute-start.12
  340.4 8.4 %collective-permute-start.11 = (f32[8,768]{1,0:T(8,128)}, f32[8,768]{1,0:T(8,128)S(1)}, u32[]{:S(2)}, u32[]{:S(2)}) collective-permute-start(f32[8,768]{1,0:T(8,128)} %fusion), channel_id=1, source_target_pairs={{0,6},{1,7},{2,8},{3,9},{4,10},{5,11},{6,12},{7,13},{8,14},{9,15},... | collective-permute-start | bytes 73736
  348.9 6.3 collective-permute-start.10
  355.3 4.4 collective-permute-start.9
  359.7 3.4 collective-permute-start.8
  365.3 4.8 collective-permute-start.6
  375.8 2.4 reshape.1814
  380.2 23.5 %concatenate.120 = f32[134,768]{1,0:T(8,128)} concatenate(f32[6,768]{1,0:T(8,128)S(1)} %copy-done.23, f32[8,768]{1,0:T(8,128)} %collective-permute-done.20, f32[8,768]{1,0:T(8,128)} %collective-permute-done.19, f32[8,768]{1,0:T(8,128)} %collective-permute-done.18, f32[8,768]{1,0:T(8,128)} %collective-permute-done.17, f32[8,768]{1,0:T(8,128)S(1)} %copy-done.25, ...), dimensions={0} | concatenate | bytes 823296
  404.5 21.8 %psum.8 = f32[6,768]{1,0:T(8,128)} all-reduce(f32[6,768]{1,0:T(8,128)S(1)} %constant_dynamic-slice_fusion), channel_id=1, replica_groups=mesh['dp'=8,'seq'=64] {'dp'}, use_global_device_ids=true, to_apply=%region_2.0 | all-reduce | flops 4608 | bytes 36864 | tf_op jit(solution)/shard_map/psum | solution.py:91
  443.1 7.5 %collective-permute-start.3 = (f32[2,128,384]{2,1,0:T(8,128)}, f32[2,128,384]{2,1,0:T(8,128)}, u32[]{:S(2)}, u32[]{:S(2)}) collective-permute-start(f32[2,128,384]{2,1,0:T(8,128)} %broadcast_select_fusion), channel_id=1, source_target_pairs={{0,4},{1,5},{2,6},{3,7},{4,0},{5,1},{6,2},{7,3},{8,12},{9,13},{10,... | collective-permute-start | bytes 1179656 | tf_op jit(solution)/shard_map/ppermute | solution.py:10
  454.8 2.6 fusion.12
  459.2 24.2 %collective-permute-done.3 = f32[2,128,384]{2,1,0:T(8,128)} collective-permute-done((f32[2,128,384]{2,1,0:T(8,128)}, f32[2,128,384]{2,1,0:T(8,128)}, u32[]{:S(2)}, u32[]{:S(2)}) %collective-permute-start.3) | collective-permute-done | bytes 393248 | tf_op jit(solution)/shard_map/ppermute | solution.py:10
  488.0 97.0 %all-reduce.11.cloned.1.call-done = f32[2,256,384]{2,1,0:T(8,128)} async-done(((f32[2,256,384]{2,1,0:T(8,128)}), f32[2,256,384]{2,1,0:T(8,128)}) %all-reduce.11.cloned.1.call-update) | async-done | bytes 786448
  593.6 2.4 reshape.1832
  602.5 2.7 collective-permute-start.5
  619.2 2.4 fusion.11
  (412 shorter events, 105.6 us)
Async XLA Ops:
  7.2 169.2 %copy-start.13 = (bf16[1,256,384]{2,1,0:T(8,128)(2,1)S(1)}, bf16[1,256,384]{2,1,0:T(8,128)(2,1)}, u32[]{:S(2)}) copy-start(bf16[1,256,384]{2,1,0:T(8,128)(2,1)} %param.103) | copy-start | bytes 589828
  7.2 577.7 %all-reduce.11.cloned.1.call-start = ((), (), s32[]{:S(2)}) async-start(), calls=%async_computation | async-start | bytes 1572864
  167.0 140.7 %collective-permute-start.20 = (f32[8,768]{1,0:T(8,128)}, f32[8,768]{1,0:T(8,128)}, u32[]{:S(2)}, u32[]{:S(2)}) collective-permute-start(f32[8,768]{1,0:T(8,128)} %fusion), channel_id=1, source_target_pairs={{0,15},{1,16},{2,17},{3,18},{4,19},{5,20},{6,21},{7,22},{8,23},{9,... | collective-permute-start | bytes 73736
  168.9 148.5 %collective-permute-start.19 = (f32[8,768]{1,0:T(8,128)}, f32[8,768]{1,0:T(8,128)}, u32[]{:S(2)}, u32[]{:S(2)}) collective-permute-start(f32[8,768]{1,0:T(8,128)} %fusion), channel_id=1, source_target_pairs={{0,14},{1,15},{2,16},{3,17},{4,18},{5,19},{6,20},{7,21},{8,22},{9,... | collective-permute-start | bytes 73736
  170.8 149.9 %collective-permute-start.18 = (f32[8,768]{1,0:T(8,128)}, f32[8,768]{1,0:T(8,128)}, u32[]{:S(2)}, u32[]{:S(2)}) collective-permute-start(f32[8,768]{1,0:T(8,128)} %fusion), channel_id=1, source_target_pairs={{0,13},{1,14},{2,15},{3,16},{4,17},{5,18},{6,19},{7,20},{8,21},{9,... | collective-permute-start | bytes 73736
  172.7 155.0 %collective-permute-start.17 = (f32[8,768]{1,0:T(8,128)}, f32[8,768]{1,0:T(8,128)}, u32[]{:S(2)}, u32[]{:S(2)}) collective-permute-start(f32[8,768]{1,0:T(8,128)} %fusion), channel_id=1, source_target_pairs={{0,12},{1,13},{2,14},{3,15},{4,16},{5,17},{6,18},{7,19},{8,20},{9,... | collective-permute-start | bytes 73736
  288.9 9.8 %collective-permute-start = (bf16[2,32,384]{2,1,0:T(8,128)(2,1)}, bf16[2,32,384]{2,1,0:T(8,128)(2,1)}, u32[]{:S(2)}, u32[]{:S(2)}) collective-permute-start(bf16[2,32,384]{2,1,0:T(8,128)(2,1)} %constant_dynamic-update-slice_fusion.16), channel_id=1, source_target_pairs={{0,1},{1,0},{2,3},{3,2},{4,5},{5,4},{6,7},{7,6},{8,9},{9,8},{10,11... | collective-permute-start | bytes 147464 | tf_op jit(solution)/shard_map/ppermute | solution.py:10
  298.7 4.5 collective-permute-start.21
  303.2 32.2 %collective-permute-start.16 = (f32[8,768]{1,0:T(8,128)}, f32[8,768]{1,0:T(8,128)S(1)}, u32[]{:S(2)}, u32[]{:S(2)}) collective-permute-start(f32[8,768]{1,0:T(8,128)} %fusion), channel_id=1, source_target_pairs={{0,11},{1,12},{2,13},{3,14},{4,15},{5,16},{6,17},{7,18},{8,19},{9,... | collective-permute-start | bytes 73736
  307.8 32.6 %collective-permute-start.15 = (f32[8,768]{1,0:T(8,128)}, f32[8,768]{1,0:T(8,128)S(1)}, u32[]{:S(2)}, u32[]{:S(2)}) collective-permute-start(f32[8,768]{1,0:T(8,128)} %fusion), channel_id=1, source_target_pairs={{0,10},{1,11},{2,12},{3,13},{4,14},{5,15},{6,16},{7,17},{8,18},{9,... | collective-permute-start | bytes 73736
  317.4 31.4 %collective-permute-start.1 = (bf16[2,64,384]{2,1,0:T(8,128)(2,1)S(1)}, bf16[2,64,384]{2,1,0:T(8,128)(2,1)S(1)}, u32[]{:S(2)}, u32[]{:S(2)}) collective-permute-start(bf16[2,64,384]{2,1,0:T(8,128)(2,1)S(1)} %maximum_select_fusion.2), channel_id=1, source_target_pairs={{0,2},{1,3},{2,0},{3,1},{4,6},{5,7},{6,4},{7,5},{8,10},{9,11},{10,... | collective-permute-start | bytes 294920 | tf_op jit(solution)/shard_map/ppermute | solution.py:10
  320.7 34.6 %collective-permute-start.14 = (f32[8,768]{1,0:T(8,128)}, f32[8,768]{1,0:T(8,128)S(1)}, u32[]{:S(2)}, u32[]{:S(2)}) collective-permute-start(f32[8,768]{1,0:T(8,128)} %fusion), channel_id=1, source_target_pairs={{0,9},{1,10},{2,11},{3,12},{4,13},{5,14},{6,15},{7,16},{8,17},{9,1... | collective-permute-start | bytes 73736
  327.7 32.0 %collective-permute-start.13 = (f32[8,768]{1,0:T(8,128)}, f32[8,768]{1,0:T(8,128)S(1)}, u32[]{:S(2)}, u32[]{:S(2)}) collective-permute-start(f32[8,768]{1,0:T(8,128)} %fusion), channel_id=1, source_target_pairs={{0,8},{1,9},{2,10},{3,11},{4,12},{5,13},{6,14},{7,15},{8,16},{9,17... | collective-permute-start | bytes 73736
  335.5 27.7 %collective-permute-start.12 = (f32[8,768]{1,0:T(8,128)}, f32[8,768]{1,0:T(8,128)S(1)}, u32[]{:S(2)}, u32[]{:S(2)}) collective-permute-start(f32[8,768]{1,0:T(8,128)} %fusion), channel_id=1, source_target_pairs={{0,7},{1,8},{2,9},{3,10},{4,11},{5,12},{6,13},{7,14},{8,15},{9,16}... | collective-permute-start | bytes 73736
  340.4 24.9 %collective-permute-start.11 = (f32[8,768]{1,0:T(8,128)}, f32[8,768]{1,0:T(8,128)S(1)}, u32[]{:S(2)}, u32[]{:S(2)}) collective-permute-start(f32[8,768]{1,0:T(8,128)} %fusion), channel_id=1, source_target_pairs={{0,6},{1,7},{2,8},{3,9},{4,10},{5,11},{6,12},{7,13},{8,14},{9,15},... | collective-permute-start | bytes 73736
  348.9 21.3 %collective-permute-start.10 = (f32[8,768]{1,0:T(8,128)}, f32[8,768]{1,0:T(8,128)S(1)}, u32[]{:S(2)}, u32[]{:S(2)}) collective-permute-start(f32[8,768]{1,0:T(8,128)} %fusion), channel_id=1, source_target_pairs={{0,5},{1,6},{2,7},{3,8},{4,9},{5,10},{6,11},{7,12},{8,13},{9,14},{... | collective-permute-start | bytes 73736
  355.3 24.8 %collective-permute-start.9 = (f32[8,768]{1,0:T(8,128)}, f32[8,768]{1,0:T(8,128)}, u32[]{:S(2)}, u32[]{:S(2)}) collective-permute-start(f32[8,768]{1,0:T(8,128)} %fusion), channel_id=1, source_target_pairs={{0,4},{1,5},{2,6},{3,7},{4,8},{5,9},{6,10},{7,11},{8,12},{9,13},{1... | collective-permute-start | bytes 73736
  359.7 20.4 %collective-permute-start.8 = (f32[8,768]{1,0:T(8,128)}, f32[8,768]{1,0:T(8,128)}, u32[]{:S(2)}, u32[]{:S(2)}) collective-permute-start(f32[8,768]{1,0:T(8,128)} %fusion), channel_id=1, source_target_pairs={{0,3},{1,4},{2,5},{3,6},{4,7},{5,8},{6,9},{7,10},{8,11},{9,12},{10... | collective-permute-start | bytes 73736
  363.2 16.9 %collective-permute-start.7 = (f32[8,768]{1,0:T(8,128)}, f32[8,768]{1,0:T(8,128)}, u32[]{:S(2)}, u32[]{:S(2)}) collective-permute-start(f32[8,768]{1,0:T(8,128)} %fusion), channel_id=1, source_target_pairs={{0,2},{1,3},{2,4},{3,5},{4,6},{5,7},{6,8},{7,9},{8,10},{9,11},{10,... | collective-permute-start | bytes 73736
  365.3 14.8 %collective-permute-start.6 = (f32[8,768]{1,0:T(8,128)}, f32[8,768]{1,0:T(8,128)}, u32[]{:S(2)}, u32[]{:S(2)}) collective-permute-start(f32[8,768]{1,0:T(8,128)} %fusion), channel_id=1, source_target_pairs={{0,1},{1,2},{2,3},{3,4},{4,5},{5,6},{6,7},{7,8},{8,9},{9,10},{10,1... | collective-permute-start | bytes 73736
  370.2 56.1 %collective-permute-start.2 = (bf16[2,128,384]{2,1,0:T(8,128)(2,1)S(1)}, bf16[2,128,384]{2,1,0:T(8,128)(2,1)}, u32[]{:S(2)}, u32[]{:S(2)}) collective-permute-start(bf16[2,128,384]{2,1,0:T(8,128)(2,1)S(1)} %maximum_select_fusion.1), channel_id=1, source_target_pairs={{0,4},{1,5},{2,6},{3,7},{4,0},{5,1},{6,2},{7,3},{8,12},{9,13},{10,... | collective-permute-start | bytes 589832 | tf_op jit(solution)/shard_map/ppermute | solution.py:10
  443.1 40.3 %collective-permute-start.3 = (f32[2,128,384]{2,1,0:T(8,128)}, f32[2,128,384]{2,1,0:T(8,128)}, u32[]{:S(2)}, u32[]{:S(2)}) collective-permute-start(f32[2,128,384]{2,1,0:T(8,128)} %broadcast_select_fusion), channel_id=1, source_target_pairs={{0,4},{1,5},{2,6},{3,7},{4,0},{5,1},{6,2},{7,3},{8,12},{9,13},{10,... | collective-permute-start | bytes 1179656 | tf_op jit(solution)/shard_map/ppermute | solution.py:10
  486.1 114.7 %collective-permute-start.4 = (f32[2,64,384]{2,1,0:T(8,128)}, f32[2,64,384]{2,1,0:T(8,128)}, u32[]{:S(2)}, u32[]{:S(2)}) collective-permute-start(f32[2,64,384]{2,1,0:T(8,128)} %slice_select_fusion), channel_id=1, source_target_pairs={{0,2},{1,3},{2,0},{3,1},{4,6},{5,7},{6,4},{7,5},{8,10},{9,11},{10,... | collective-permute-start | bytes 589832 | tf_op jit(solution)/shard_map/ppermute | solution.py:10
  602.5 7.9 %collective-permute-start.5 = (f32[2,32,384]{2,1,0:T(8,128)S(1)}, f32[2,32,384]{2,1,0:T(8,128)S(1)}, u32[]{:S(2)}, u32[]{:S(2)}) collective-permute-start(f32[2,32,384]{2,1,0:T(8,128)S(1)} %slice_select_fusion.1), channel_id=1, source_target_pairs={{0,1},{1,0},{2,3},{3,2},{4,5},{5,4},{6,7},{7,6},{8,9},{9,8},{10,11... | collective-permute-start | bytes 294920 | tf_op jit(solution)/shard_map/ppermute | solution.py:10
  (43 other events, 1665.5 us)
Sparse Core Ops, SparseCore 0:
  286.1 298.8 all-reduce.10
where the time goes:
time: 636 us; the launch traced here: 633 us
  blocking collectives  279 us (44%)
  waiting for transfers between devices  122 us (19%)
  local copies, waits for them, and re-layouts  96.5 us (15%)
  starting transfers between devices  92.8 us (15%)
  matrix products  17.9 us (3%)
  between operations  16.9 us (3%)
  other arithmetic  8.05 us (1%)
    unnamed x1, blocking collectives  158 us
    all_gather x1, blocking collectives, on_device(): far_remote = lax.all_gather(far_pair, 'seq', axis=1, tiled=True)  98.5 us
    unnamed x18, waiting for transfers between devices  97.6 us
    unnamed x17, starting transfers between devices  74 us
    unnamed x208, local copies, waits for them, and re-layouts  38 us
    ppermute x6, waiting for transfers between devices, swapped(): lax.ppermute(shard, axis, [(i, i ^ 1 << distance) for i in range(lax.axis...  24.2 us
    scatter x54, local copies, waits for them, and re-layouts, place(): shaped = shaped.at[:, h % stride, h, :].set(y[:, h, :])  23.4 us
    psum x1, blocking collectives, on_device(): summed = lax.psum(full, 'dp')  21.8 us
  transfers between devices with their start and end apart: 23, of which 3 were waited for; matrix products, arithmetic and copies ran while one was open for 16% of the time, Pallas kernels for 0%

commit v1 on v0

--- a/solution.py
+++ b/solution.py
@@ -88,7 +88,7 @@
     full = lax.dot_general(
         output2, upstream, (((0,), (0,)), ((), ())), preferred_element_type=jnp.float32
     )
-    summed = lax.psum(full, "dp")
+    summed = jnp.sum(lax.all_gather(full, "dp"), axis=0)
     grad_weight = lax.psum_scatter(summed, "seq", scatter_dimension=0, tiled=True)
     dq0, dk0, dv0 = set_backward(query3, dout3, lse, delta, key3, value3, scale)
     total_q = dq0

time: 636 us -> 691 us (1.086)
  waiting for transfers between devices: 122 us -> 219 us
  blocking collectives: 279 us -> 252 us
  local copies, waits for them, and re-layouts: 96.5 us -> 86.3 us
  starting transfers between devices: 92.8 us -> 82.8 us
    unnamed x18 -> x19, waiting for transfers between devices: 97.6 us -> 185 us
    psum x1 -> x0, blocking collectives: 21.8 us -> none  [on_device(): summed = lax.psum(full, 'dp')]
    unnamed x208 -> x202, local copies, waits for them, and re-layouts: 38 us -> 20.3 us
    ppermute x6, waiting for transfers between devices: 24.2 us -> 34.2 us  [swapped(): lax.ppermute(shard, axis, [(i, i ^ 1 << distance) for i in range(lax.axis...]
    unnamed x17, starting transfers between devices: 74 us -> 64.2 us
    unnamed x1, blocking collectives: 158 us -> 151 us
  transfers between devices with their start and end apart: 23 -> 24, of which waited for: 3 -> 3; matrix products, arithmetic and copies ran while one was open for 16% -> 13% of each run, Pallas kernels for 0% -> 0%
where the time goes in v1:
time: 691 us; the launch traced here: 689 us
  blocking collectives  252 us (36%)
  waiting for transfers between devices  219 us (32%)
  local copies, waits for them, and re-layouts  86.3 us (12%)
  starting transfers between devices  82.8 us (12%)
  matrix products  19.5 us (3%)
  between operations  18.2 us (3%)
  other arithmetic  11.2 us (2%)
    unnamed x19, waiting for transfers between devices  185 us
    unnamed x1, blocking collectives  151 us
    all_gather x1, blocking collectives, on_device(): far_remote = lax.all_gather(far_pair, 'seq', axis=1, tiled=True)  101 us
    unnamed x17, starting transfers between devices  64.2 us
    ppermute x6, waiting for transfers between devices, swapped(): lax.ppermute(shard, axis, [(i, i ^ 1 << distance) for i in range(lax.axis...  34.2 us
    scatter x54, local copies, waits for them, and re-layouts, place(): shaped = shaped.at[:, h % stride, h, :].set(y[:, h, :])  28.6 us
    unnamed x202, local copies, waits for them, and re-layouts  20.3 us
    ppermute x6, starting transfers between devices, swapped(): lax.ppermute(shard, axis, [(i, i ^ 1 << distance) for i in range(lax.axis...  18.6 us
  transfers between devices with their start and end apart: 24, of which 3 were waited for; matrix products, arithmetic and copies ran while one was open for 13% of the time, Pallas kernels for 0%

profile of v1, /device:TPU:8, one launch (start us, length us, event | category | flops | bytes accessed | tf_op | source)
XLA Modules:
  0.0 688.8 jit_solution(17704049961161242861)
XLA Ops:
  15.3 101.3 %all_gather.9 = bf16[2,256,384]{2,0,1:T(2,128)(2,1)S(1)} all-gather(bf16[2,4,384]{2,0,1:T(2,128)(2,1)S(1)} %copy.1023), channel_id=1, replica_groups=mesh['dp'=8,'seq'=64] {'seq'}, dimensions={1}, use_global_device_ids=true | all-gather | bytes 399360 | tf_op jit(solution)/shard_map/all_gather | solution.py:129
  141.1 4.8 collective-permute-start.1
  147.0 2.4 copy.1056
  149.4 2.4 reshape.1814
  153.7 5.4 collective-permute-start.2
  159.2 28.1 %collective-permute-done.2 = bf16[2,128,384]{2,1,0:T(8,128)(2,1)S(1)} collective-permute-done((bf16[2,128,384]{2,1,0:T(8,128)(2,1)S(1)}, bf16[2,128,384]{2,1,0:T(8,128)(2,1)S(1)}, u32[]{:S(2)}, u32[]{:S(2)}) %collective-permute-start.2) | collective-permute-done | bytes 196640 | tf_op jit(solution)/shard_map/ppermute | solution.py:10
  210.1 2.6 fusion.12
  214.5 6.1 collective-permute-done.3
  225.1 184.7 %all-reduce.11.cloned.1.call-done = f32[2,256,384]{2,1,0:T(8,128)} async-done(((f32[2,256,384]{2,1,0:T(8,128)}), f32[2,256,384]{2,1,0:T(8,128)}) %all-reduce.11.cloned.1.call-update) | async-done | bytes 786448
  415.9 2.3 copy.1066
  418.3 2.4 reshape.1850
  427.1 2.7 collective-permute-start.5
  430.3 2.3 copy.1063
  432.7 2.3 reshape.1832
  437.1 2.3 copy.1065
  448.1 4.4 reduce_sum.19
  452.5 150.5 %fusion = f32[8,768]{1,0:T(8,128)S(1)} fusion(f32[384,768]{1,0:T(8,128)S(1)} %reduce_sum.19), kind=kCustom, calls=%all-reduce-scatter | all-reduce-scatter fusion | flops 393217 | bytes 1206272
  610.4 8.7 %collective-permute-start.14 = (f32[8,768]{1,0:T(8,128)S(1)}, f32[8,768]{1,0:T(8,128)S(1)}, u32[]{:S(2)}, u32[]{:S(2)}) collective-permute-start(f32[8,768]{1,0:T(8,128)S(1)} %fusion), channel_id=1, source_target_pairs={{0,9},{1,10},{2,11},{3,12},{4,13},{5,14},{6,15},{7,16},{8,17},{9,1... | collective-permute-start | bytes 73736
  619.6 23.5 %collective-permute-start.15 = (f32[8,768]{1,0:T(8,128)S(1)}, f32[8,768]{1,0:T(8,128)}, u32[]{:S(2)}, u32[]{:S(2)}) collective-permute-start(f32[8,768]{1,0:T(8,128)S(1)} %fusion), channel_id=1, source_target_pairs={{0,10},{1,11},{2,12},{3,13},{4,14},{5,15},{6,16},{7,17},{8,18},{9,... | collective-permute-start | bytes 73736
  645.3 4.6 collective-permute-start.17
  658.7 2.5 collective-permute-start.6
  663.2 6.2 collective-permute-start.8
  669.5 2.8 collective-permute-start.9
  675.3 5.4 concatenate.120
  (409 shorter events, 109.8 us)
Async XLA Ops:
  8.0 401.8 %all-reduce.11.cloned.1.call-start = ((), (), s32[]{:S(2)}) async-start(), calls=%async_computation.1 | async-start | bytes 1572864
  125.1 323.0 %all-gather.3.cloned.1.call-start = ((), (), s32[]{:S(2)}) async-start(), calls=%async_computation | async-start | bytes 10616832 | tf_op jit(solution)/shard_map/all_gather | solution.py:91
  130.0 10.1 %collective-permute-start = (bf16[2,32,384]{2,1,0:T(8,128)(2,1)}, bf16[2,32,384]{2,1,0:T(8,128)(2,1)}, u32[]{:S(2)}, u32[]{:S(2)}) collective-permute-start(bf16[2,32,384]{2,1,0:T(8,128)(2,1)} %constant_dynamic-update-slice_fusion.16), channel_id=1, source_target_pairs={{0,1},{1,0},{2,3},{3,2},{4,5},{5,4},{6,7},{7,6},{8,9},{9,8},{10,11... | collective-permute-start | bytes 147464 | tf_op jit(solution)/shard_map/ppermute | solution.py:10
  141.1 12.6 %collective-permute-start.1 = (bf16[2,64,384]{2,1,0:T(8,128)(2,1)S(1)}, bf16[2,64,384]{2,1,0:T(8,128)(2,1)S(1)}, u32[]{:S(2)}, u32[]{:S(2)}) collective-permute-start(bf16[2,64,384]{2,1,0:T(8,128)(2,1)S(1)} %maximum_select_fusion.2), channel_id=1, source_target_pairs={{0,2},{1,3},{2,0},{3,1},{4,6},{5,7},{6,4},{7,5},{8,10},{9,11},{10,... | collective-permute-start | bytes 294920 | tf_op jit(solution)/shard_map/ppermute | solution.py:10
  153.7 33.6 %collective-permute-start.2 = (bf16[2,128,384]{2,1,0:T(8,128)(2,1)S(1)}, bf16[2,128,384]{2,1,0:T(8,128)(2,1)S(1)}, u32[]{:S(2)}, u32[]{:S(2)}) collective-permute-start(bf16[2,128,384]{2,1,0:T(8,128)(2,1)S(1)} %maximum_select_fusion.1), channel_id=1, source_target_pairs={{0,4},{1,5},{2,6},{3,7},{4,0},{5,1},{6,2},{7,3},{8,12},{9,13},{10,... | collective-permute-start | bytes 589832 | tf_op jit(solution)/shard_map/ppermute | solution.py:10
  202.8 17.7 %collective-permute-start.3 = (f32[2,128,384]{2,1,0:T(8,128)}, f32[2,128,384]{2,1,0:T(8,128)}, u32[]{:S(2)}, u32[]{:S(2)}) collective-permute-start(f32[2,128,384]{2,1,0:T(8,128)} %broadcast_select_fusion), channel_id=1, source_target_pairs={{0,4},{1,5},{2,6},{3,7},{4,0},{5,1},{6,2},{7,3},{8,12},{9,13},{10,... | collective-permute-start | bytes 1179656 | tf_op jit(solution)/shard_map/ppermute | solution.py:10
  223.2 202.2 %collective-permute-start.4 = (f32[2,64,384]{2,1,0:T(8,128)}, f32[2,64,384]{2,1,0:T(8,128)}, u32[]{:S(2)}, u32[]{:S(2)}) collective-permute-start(f32[2,64,384]{2,1,0:T(8,128)} %slice_select_fusion), channel_id=1, source_target_pairs={{0,2},{1,3},{2,0},{3,1},{4,6},{5,7},{6,4},{7,5},{8,10},{9,11},{10,... | collective-permute-start | bytes 589832 | tf_op jit(solution)/shard_map/ppermute | solution.py:10
  427.1 7.9 %collective-permute-start.5 = (f32[2,32,384]{2,1,0:T(8,128)S(1)}, f32[2,32,384]{2,1,0:T(8,128)S(1)}, u32[]{:S(2)}, u32[]{:S(2)}) collective-permute-start(f32[2,32,384]{2,1,0:T(8,128)S(1)} %slice_select_fusion.1), channel_id=1, source_target_pairs={{0,1},{1,0},{2,3},{3,2},{4,5},{5,4},{6,7},{7,6},{8,9},{9,8},{10,11... | collective-permute-start | bytes 294920 | tf_op jit(solution)/shard_map/ppermute | solution.py:10
  603.1 7.2 %collective-permute-start.21 = (f32[6,768]{1,0:T(8,128)S(1)}, f32[6,768]{1,0:T(8,128)S(1)}, u32[]{:S(2)}, u32[]{:S(2)}) collective-permute-start(f32[6,768]{1,0:T(8,128)S(1)} %slice.2078), channel_id=1, source_target_pairs={{0,16},{1,17},{2,18},{3,19},{4,20},{5,21},{6,22},{7,23},{8,24},{9,... | collective-permute-start | bytes 55304
  605.2 14.5 %collective-permute-start.10 = (f32[8,768]{1,0:T(8,128)S(1)}, f32[8,768]{1,0:T(8,128)S(1)}, u32[]{:S(2)}, u32[]{:S(2)}) collective-permute-start(f32[8,768]{1,0:T(8,128)S(1)} %fusion), channel_id=1, source_target_pairs={{0,5},{1,6},{2,7},{3,8},{4,9},{5,10},{6,11},{7,12},{8,13},{9,14},{... | collective-permute-start | bytes 73736
  606.5 36.7 %collective-permute-start.11 = (f32[8,768]{1,0:T(8,128)S(1)}, f32[8,768]{1,0:T(8,128)S(1)}, u32[]{:S(2)}, u32[]{:S(2)}) collective-permute-start(f32[8,768]{1,0:T(8,128)S(1)} %fusion), channel_id=1, source_target_pairs={{0,6},{1,7},{2,8},{3,9},{4,10},{5,11},{6,12},{7,13},{8,14},{9,15},... | collective-permute-start | bytes 73736
  607.8 37.5 %collective-permute-start.12 = (f32[8,768]{1,0:T(8,128)S(1)}, f32[8,768]{1,0:T(8,128)S(1)}, u32[]{:S(2)}, u32[]{:S(2)}) collective-permute-start(f32[8,768]{1,0:T(8,128)S(1)} %fusion), channel_id=1, source_target_pairs={{0,7},{1,8},{2,9},{3,10},{4,11},{5,12},{6,13},{7,14},{8,15},{9,16}... | collective-permute-start | bytes 73736
  609.1 40.8 %collective-permute-start.13 = (f32[8,768]{1,0:T(8,128)S(1)}, f32[8,768]{1,0:T(8,128)S(1)}, u32[]{:S(2)}, u32[]{:S(2)}) collective-permute-start(f32[8,768]{1,0:T(8,128)S(1)} %fusion), channel_id=1, source_target_pairs={{0,8},{1,9},{2,10},{3,11},{4,12},{5,13},{6,14},{7,15},{8,16},{9,17... | collective-permute-start | bytes 73736
  610.4 41.4 %collective-permute-start.14 = (f32[8,768]{1,0:T(8,128)S(1)}, f32[8,768]{1,0:T(8,128)S(1)}, u32[]{:S(2)}, u32[]{:S(2)}) collective-permute-start(f32[8,768]{1,0:T(8,128)S(1)} %fusion), channel_id=1, source_target_pairs={{0,9},{1,10},{2,11},{3,12},{4,13},{5,14},{6,15},{7,16},{8,17},{9,1... | collective-permute-start | bytes 73736
  619.6 37.6 %collective-permute-start.15 = (f32[8,768]{1,0:T(8,128)S(1)}, f32[8,768]{1,0:T(8,128)}, u32[]{:S(2)}, u32[]{:S(2)}) collective-permute-start(f32[8,768]{1,0:T(8,128)S(1)} %fusion), channel_id=1, source_target_pairs={{0,10},{1,11},{2,12},{3,13},{4,14},{5,15},{6,16},{7,17},{8,18},{9,... | collective-permute-start | bytes 73736
  643.2 15.5 %collective-permute-start.16 = (f32[8,768]{1,0:T(8,128)S(1)}, f32[8,768]{1,0:T(8,128)}, u32[]{:S(2)}, u32[]{:S(2)}) collective-permute-start(f32[8,768]{1,0:T(8,128)S(1)} %fusion), channel_id=1, source_target_pairs={{0,11},{1,12},{2,13},{3,14},{4,15},{5,16},{6,17},{7,18},{8,19},{9,... | collective-permute-start | bytes 73736
  645.3 15.9 %collective-permute-start.17 = (f32[8,768]{1,0:T(8,128)S(1)}, f32[8,768]{1,0:T(8,128)}, u32[]{:S(2)}, u32[]{:S(2)}) collective-permute-start(f32[8,768]{1,0:T(8,128)S(1)} %fusion), channel_id=1, source_target_pairs={{0,12},{1,13},{2,14},{3,15},{4,16},{5,17},{6,18},{7,19},{8,20},{9,... | collective-permute-start | bytes 73736
  649.8 13.4 %collective-permute-start.18 = (f32[8,768]{1,0:T(8,128)S(1)}, f32[8,768]{1,0:T(8,128)}, u32[]{:S(2)}, u32[]{:S(2)}) collective-permute-start(f32[8,768]{1,0:T(8,128)S(1)} %fusion), channel_id=1, source_target_pairs={{0,13},{1,14},{2,15},{3,16},{4,17},{5,18},{6,19},{7,20},{8,21},{9,... | collective-permute-start | bytes 73736
  651.7 17.7 %collective-permute-start.19 = (f32[8,768]{1,0:T(8,128)S(1)}, f32[8,768]{1,0:T(8,128)}, u32[]{:S(2)}, u32[]{:S(2)}) collective-permute-start(f32[8,768]{1,0:T(8,128)S(1)} %fusion), channel_id=1, source_target_pairs={{0,14},{1,15},{2,16},{3,17},{4,18},{5,19},{6,20},{7,21},{8,22},{9,... | collective-permute-start | bytes 73736
  657.2 18.0 %collective-permute-start.20 = (f32[8,768]{1,0:T(8,128)S(1)}, f32[8,768]{1,0:T(8,128)S(1)}, u32[]{:S(2)}, u32[]{:S(2)}) collective-permute-start(f32[8,768]{1,0:T(8,128)S(1)} %fusion), channel_id=1, source_target_pairs={{0,15},{1,16},{2,17},{3,18},{4,19},{5,20},{6,21},{7,22},{8,23},{9,... | collective-permute-start | bytes 73736
  658.7 16.5 %collective-permute-start.6 = (f32[8,768]{1,0:T(8,128)S(1)}, f32[8,768]{1,0:T(8,128)S(1)}, u32[]{:S(2)}, u32[]{:S(2)}) collective-permute-start(f32[8,768]{1,0:T(8,128)S(1)} %fusion), channel_id=1, source_target_pairs={{0,1},{1,2},{2,3},{3,4},{4,5},{5,6},{6,7},{7,8},{8,9},{9,10},{10,1... | collective-permute-start | bytes 73736
  661.2 14.1 %collective-permute-start.7 = (f32[8,768]{1,0:T(8,128)S(1)}, f32[8,768]{1,0:T(8,128)S(1)}, u32[]{:S(2)}, u32[]{:S(2)}) collective-permute-start(f32[8,768]{1,0:T(8,128)S(1)} %fusion), channel_id=1, source_target_pairs={{0,2},{1,3},{2,4},{3,5},{4,6},{5,7},{6,8},{7,9},{8,10},{9,11},{10,... | collective-permute-start | bytes 73736
  663.2 12.0 %collective-permute-start.8 = (f32[8,768]{1,0:T(8,128)S(1)}, f32[8,768]{1,0:T(8,128)S(1)}, u32[]{:S(2)}, u32[]{:S(2)}) collective-permute-start(f32[8,768]{1,0:T(8,128)S(1)} %fusion), channel_id=1, source_target_pairs={{0,3},{1,4},{2,5},{3,6},{4,7},{5,8},{6,9},{7,10},{8,11},{9,12},{10... | collective-permute-start | bytes 73736
  669.5 5.8 collective-permute-start.9
  (41 other events, 863.3 us)
Sparse Core Ops, SparseCore 0:
  125.3 284.5 all-reduce.10
Sparse Core Ops, SparseCore 1:
  133.5 56.7 all-gather.2
